TPU v7x, 32 devices: a whole 2x2x4 slice. The times are simulated.
32 devices in a mesh: wide: 8 (over z, y), lev: 4 (over x, core).
Axes of the slice: x: 2, y: 2, z: 4, core: 2. Of those that a mesh axis runs over, the one named last changes fastest.
Arguments:
- nonlinear: bfloat16 [3, 2, 256, 8, 4096], P(None, None, 'lev', None, 'wide'), may hold values from -20 to 20
Outputs:
- pressure: float32 [2, 256, 8, 1536], P(None, 'lev', 'wide')
All inputs are finite; a program needn't handle non-finite values.
Results may differ from a plain program's by a relative error of at most 0.0034.
Values may be sent and summed in bfloat16 or wider, within the bound.
A program may use at most 64 MiB of HBM per device.

v0:
```python
import functools
import math

import jax
import jax.numpy as jnp
import ml_dtypes
import numpy as np
from jax import lax
from jax.experimental import pallas as pl
from jax.experimental.pallas import tpu as pltpu
from jax.sharding import PartitionSpec as P

NXG = 4096
KXM = 1536
MESH = pl.DeviceIdType.MESH
COLS = 512


def make_tables():
    places = np.arange(NXG, dtype=np.int32)
    waves = np.arange(KXM, dtype=np.int32) - KXM // 2
    phases = np.mod(places[:, None] * waves[None, :], NXG)
    turn = np.arange(NXG, dtype=np.float32) * np.float32(2.0 * math.pi / NXG)
    cosine = np.cos(turn).astype(ml_dtypes.bfloat16)[phases]
    sine = np.sin(turn).astype(ml_dtypes.bfloat16)[phases]
    return np.concatenate([cosine, sine], axis=1)


def partner(me, step, count):
    total, unit = 0, 1
    while unit < count:
        total = total + unit * ((me // unit + step // unit) % 2)
        unit *= 2
    return total


def kernel(
    wide, lev, rows_ky, levels,
    x_ref, tab_ref, out_ref,
    tab, send, recv, halo_lo, halo_hi, zpad, acc, coef, from_lo, from_hi, part, dense,
    ends, last_val, first_val,
    tab_sem, halo_send, halo_recv, send_sem, recv_sem, end_send, end_recv,
):
    chunk = x_ref.shape[3]
    line_rows = levels * rows_ky
    half = 2 * levels
    group_levels = max(16, 256 // rows_ky)
    group_rows = group_levels * rows_ky
    groups = levels // group_levels
    halo_rows = halo_lo.shape[1]
    me = lax.axis_index("wide")
    block = lax.axis_index("lev")

    tab_parts = tab_sem.shape[0]
    tab_rows = NXG // tab_parts

    def tab_copy(i):
        rows = pl.ds(i * tab_rows, tab_rows)
        return pltpu.make_async_copy(tab_ref.at[rows], tab.at[rows], tab_sem.at[i])

    barrier = pltpu.get_barrier_semaphore()
    for step in range(1, wide):
        pl.semaphore_signal(
            barrier, inc=1, device_id={"wide": partner(me, step, wide)}, device_id_type=MESH
        )
    for step in range(1, lev):
        pl.semaphore_signal(
            barrier, inc=1, device_id={"lev": (block + step) % lev}, device_id_type=MESH
        )
    out_row = lax.broadcasted_iota(jnp.int32, (group_rows, group_rows), 0)
    in_row = lax.broadcasted_iota(jnp.int32, (group_rows, group_rows), 1)
    wanted = (out_row % group_levels) * rows_ky + out_row // group_levels
    shuffle = jnp.where(in_row == wanted, 1.0, 0.0).astype(jnp.bfloat16)

    def place(values, first):
        moved = jnp.dot(shuffle, values, preferred_element_type=jnp.float32).astype(jnp.bfloat16)
        for ky in range(rows_ky):
            send[ky, first:first + group_levels, :] = moved[
                ky * group_levels:(ky + 1) * group_levels
            ]

    def line_copy(step, which):
        other = partner(me, step, wide)
        rows = pl.ds(which * half, half)
        return pltpu.make_async_remote_copy(
            src_ref=send.at[other, rows],
            dst_ref=recv.at[me, rows],
            send_sem=send_sem.at[which, step],
            recv_sem=recv_sem.at[which, step],
            device_id={"wide": other},
            device_id_type=MESH,
        )

    def line_arrival(step, which):
        other = partner(me, step, wide)
        rows = pl.ds(which * half, half)
        return pltpu.make_async_remote_copy(
            src_ref=send.at[other, rows],
            dst_ref=recv.at[other, rows],
            send_sem=send_sem.at[which, step],
            recv_sem=recv_sem.at[which, step],
            device_id={"wide": other},
            device_id_type=MESH,
        )

    for c in range(2):
        for g in range(groups):
            place(
                x_ref[0, c, g * group_rows:(g + 1) * group_rows, :],
                c * levels + g * group_levels,
            )
    pl.semaphore_wait(barrier, wide + lev - 2)

    to_prev = pltpu.make_async_remote_copy(
        src_ref=x_ref.at[2, :, 0:halo_rows],
        dst_ref=halo_hi,
        send_sem=halo_send.at[0],
        recv_sem=halo_recv.at[0],
        device_id={"lev": (block + lev - 1) % lev},
        device_id_type=MESH,
    )
    to_next = pltpu.make_async_remote_copy(
        src_ref=x_ref.at[2, :, line_rows - halo_rows:line_rows],
        dst_ref=halo_lo,
        send_sem=halo_send.at[1],
        recv_sem=halo_recv.at[1],
        device_id={"lev": (block + 1) % lev},
        device_id_type=MESH,
    )
    to_prev.start()
    to_next.start()

    quarter = wide // 4
    same = (me // (2 * quarter) + me // quarter + 1) % 2
    end_steps = [2 * quarter + same * quarter + i for i in range(quarter)]
    mid_steps = [2 * quarter + (1 - same) * quarter + i for i in range(quarter)]
    near_steps = range(wide // 2 - 1, 0, -1)
    for step in end_steps:
        line_copy(step, 0).start()

    for i in range(tab_parts):
        tab_copy(i).start()

    for c in range(2):
        zpad[c, rows_ky:rows_ky + line_rows, :] = x_ref[2, c].astype(jnp.float32)
    to_prev.wait_recv()
    to_next.wait_recv()
    for c in range(2):
        low = halo_lo[c].astype(jnp.float32)[halo_rows - rows_ky:]
        high = halo_hi[c].astype(jnp.float32)[:rows_ky]
        zpad[c, 0:rows_ky, :] = jnp.where(block > 0, low, 0.0)
        zpad[c, rows_ky + line_rows:, :] = jnp.where(block < lev - 1, high, 0.0)
    spacing = 2.0 * math.pi / NXG
    ky_row = lax.broadcasted_iota(jnp.int32, (group_rows, chunk), 0) % rows_ky
    ky_scaled = ky_row.astype(jnp.float32) * spacing
    for c in range(2):
        for g in range(groups):
            at = g * group_rows
            upper = zpad[c, at + 2 * rows_ky:at + 2 * rows_ky + group_rows, :]
            lower = zpad[c, at:at + group_rows, :]
            turned = ky_scaled * x_ref[1, 1 - c, at:at + group_rows, :].astype(jnp.float32)
            slope = (upper - lower) * 0.5
            mixed = slope - turned if c == 0 else slope + turned
            place(mixed.astype(jnp.bfloat16), half + c * levels + g * group_levels)
    for step in end_steps:
        line_copy(step, 1).start()
    for steps in (mid_steps, near_steps):
        for step in steps:
            line_copy(step, 0).start()
            line_copy(step, 1).start()

    kx_scaled = (
        lax.broadcasted_iota(jnp.int32, (1, KXM), 1) - KXM // 2
    ).astype(jnp.float32) * spacing
    ky_here = me.astype(jnp.float32) * spacing
    diagonal = 2.0 + (ky_here * ky_here + kx_scaled * kx_scaled)

    def coef_step(i, carry):
        shift, gain = carry
        inverse = 1.0 / (diagonal - shift)
        gain = gain * inverse
        coef[pl.ds(i, 1), :] = inverse
        from_lo[pl.ds(i, 1), :] = gain
        return inverse, gain

    zeros = jnp.zeros((1, KXM), jnp.float32)
    ones = jnp.ones((1, KXM), jnp.float32)
    lax.fori_loop(0, levels, coef_step, (zeros, ones))

    def unit_step(j, carry):
        i = levels - 1 - j
        low, high = carry
        inverse = coef[pl.ds(i, 1), :]
        low = from_lo[pl.ds(i, 1), :] + inverse * low
        high = inverse * high
        from_lo[pl.ds(i, 1), :] = low
        from_hi[pl.ds(i, 1), :] = high
        return low, high

    lax.fori_loop(0, levels, unit_step, (zeros, ones))

    tiles = KXM // 128
    deep = 2 * tiles
    for j in range(tiles):
        column = coef[:, j * 128:(j + 1) * 128]
        for c in range(2):
            dense[pl.ds(c * tiles + j, levels, stride=deep), :] = column

    for i in range(tab_parts):
        tab_copy(i).wait()

    own_at = pl.multiple_of(me * chunk, chunk)

    @pl.loop(0, 2 * KXM // COLS)
    def _(t):
        cols = pl.ds(pl.multiple_of(t * COLS, COLS), COLS)
        acc[:, cols] = jnp.dot(
            send[me], tab[pl.ds(own_at, chunk), cols], preferred_element_type=jnp.float32
        )

    def chunk_step(step, carry):
        line_arrival(step, 0).wait_recv()
        line_arrival(step, 1).wait_recv()
        other = partner(me, step, wide)
        rows = pl.ds(pl.multiple_of(other * chunk, chunk), chunk)

        @pl.loop(0, 2 * KXM // COLS)
        def _(t):
            cols = pl.ds(pl.multiple_of(t * COLS, COLS), COLS)
            acc[:, cols] += jnp.dot(
                recv[other], tab[rows, cols], preferred_element_type=jnp.float32
            )

        return carry

    lax.fori_loop(1, wide - 1, chunk_step, 0)

    line_arrival(wide - 1, 0).wait_recv()
    line_arrival(wide - 1, 1).wait_recv()
    last = partner(me, wide - 1, wide)
    last_rows = pl.ds(pl.multiple_of(last * chunk, chunk), chunk)
    norm_scale = 1.0 / math.sqrt(NXG)

    @pl.loop(0, KXM // 256)
    def _(t):
        cc = pl.ds(pl.multiple_of(t * 256, 256), 256)
        ss = pl.ds(pl.multiple_of(KXM + t * 256, 256), 256)
        lines = recv[last]
        with_cos = acc[:, cc] + jnp.dot(
            lines, tab[last_rows, cc], preferred_element_type=jnp.float32
        )
        with_sin = acc[:, ss] + jnp.dot(
            lines, tab[last_rows, ss], preferred_element_type=jnp.float32
        )
        kx = (
            lax.broadcasted_iota(jnp.int32, (1, 256), 1) + t * 256 - KXM // 2
        ).astype(jnp.float32) * spacing
        n = levels
        fx_real = (with_cos[0:n] + with_sin[n:2 * n]) * norm_scale
        fx_imag = (with_cos[n:2 * n] - with_sin[0:n]) * norm_scale
        fg_real = (with_cos[2 * n:3 * n] + with_sin[3 * n:4 * n]) * norm_scale
        fg_imag = (with_cos[3 * n:4 * n] - with_sin[2 * n:3 * n]) * norm_scale
        source_real = kx * fx_imag - fg_real
        source_imag = -kx * fx_real - fg_imag
        for j in range(2):
            at = slice(j * 128, (j + 1) * 128)
            part[pl.ds(2 * t + j, n, stride=deep), :] = source_real[:, at]
            part[pl.ds(tiles + 2 * t + j, n, stride=deep), :] = source_imag[:, at]
        low, high = from_lo[:, cc], from_hi[:, cc]
        ends[block, 0:1, cc] = jnp.sum(low * source_real, axis=0, keepdims=True)
        ends[block, 1:2, cc] = jnp.sum(low * source_imag, axis=0, keepdims=True)
        ends[block, 2:3, cc] = jnp.sum(high * source_real, axis=0, keepdims=True)
        ends[block, 3:4, cc] = jnp.sum(high * source_imag, axis=0, keepdims=True)

    def end_copy(step, slot):
        return pltpu.make_async_remote_copy(
            src_ref=ends.at[slot],
            dst_ref=ends.at[slot],
            send_sem=end_send.at[step],
            recv_sem=end_recv.at[step],
            device_id={"lev": (block + step) % lev},
            device_id_type=MESH,
        )

    for step in range(1, lev):
        end_copy(step, block).start()

    def down_step(i, carry):
        rows = pl.ds(pl.multiple_of(i * deep, 8), deep)
        value = (part[rows, :] + carry) * dense[rows, :]
        part[rows, :] = value
        return value

    zero_level = jnp.zeros((deep, 128), jnp.float32)
    lax.fori_loop(0, levels, down_step, zero_level, unroll=8)

    def up_step(j, carry):
        rows = pl.ds(pl.multiple_of((levels - 1 - j) * deep, 8), deep)
        value = part[rows, :] + dense[rows, :] * carry
        part[rows, :] = value
        return value

    lax.fori_loop(0, levels, up_step, zero_level, unroll=8)

    for step in range(1, lev):
        end_copy(step, (block + lev - step) % lev).wait_recv()

    near, far = from_lo[0:1, :], from_lo[levels - 1:levels, :]
    value, ratio = ends[0, 2:4, :], near
    values, ratios, inverses = [value], [ratio], [None]
    for b in range(1, lev):
        inverse = 1.0 / (1.0 - near * ratio)
        lead = far * ratio * inverse
        first = ends[b, 0:2, :] + near * value
        value = ends[b, 2:4, :] + far * value + lead * first
        ratio = near + lead * far
        values.append(value)
        ratios.append(ratio)
        inverses.append(inverse)
    follow = jnp.zeros((2, KXM), jnp.float32)
    first_val[lev] = follow
    last_val[0] = follow
    for b in range(lev - 1, 0, -1):
        follow = inverses[b] * (ends[b, 0:2, :] + near * values[b - 1] + far * follow)
        first_val[b] = follow
        last_val[b] = values[b - 1] + ratios[b - 1] * follow
    below = last_val[block]
    above = first_val[block + 1]
    for c in range(2):
        for j in range(tiles):
            at = slice(j * 128, (j + 1) * 128)
            solved = (
                part[pl.ds(c * tiles + j, levels, stride=deep), :]
                + from_lo[:, at] * below[c:c + 1, at]
                + from_hi[:, at] * above[c:c + 1, at]
            )
            out_ref[pl.ds(c * levels * tiles + j, levels, stride=tiles), :] = solved

    to_prev.wait_send()
    to_next.wait_send()
    for step in range(1, wide):
        line_copy(step, 0).wait_send()
        line_copy(step, 1).wait_send()
    for step in range(1, lev):
        end_copy(step, block).wait_send()


def hand_over(x_ref, out_ref):
    out_ref[...] = x_ref[...]


def solution(mesh):
    wide, lev = mesh.shape["wide"], mesh.shape["lev"]
    tables = make_tables()

    def local(nonlinear):
        _, _, levels, rows_ky, chunk = nonlinear.shape
        rows = levels * rows_ky
        halo_rows = max(16, rows_ky)
        f32, bf16 = jnp.float32, jnp.bfloat16
        dma = pltpu.SemaphoreType.DMA
        pressure = pl.pallas_call(
            functools.partial(kernel, wide, lev, rows_ky, levels),
            out_shape=jax.ShapeDtypeStruct((2 * levels * KXM // 128, 128), f32),
            in_specs=[
                pl.BlockSpec(memory_space=pltpu.VMEM),
                pl.BlockSpec(memory_space=pl.ANY),
            ],
            out_specs=pl.BlockSpec(memory_space=pltpu.VMEM),
            scratch_shapes=[
                pltpu.VMEM((NXG, 2 * KXM), bf16),
                pltpu.VMEM((wide, 4 * levels, chunk), bf16),
                pltpu.VMEM((wide, 4 * levels, chunk), bf16),
                pltpu.VMEM((2, halo_rows, chunk), bf16),
                pltpu.VMEM((2, halo_rows, chunk), bf16),
                pltpu.VMEM((2, rows + 2 * rows_ky, chunk), f32),
                pltpu.VMEM((4 * levels, 2 * KXM), f32),
                pltpu.VMEM((levels, KXM), f32),
                pltpu.VMEM((levels, KXM), f32),
                pltpu.VMEM((levels, KXM), f32),
                pltpu.VMEM((2 * levels * KXM // 128, 128), f32),
                pltpu.VMEM((2 * levels * KXM // 128, 128), f32),
                pltpu.VMEM((lev, 8, KXM), f32),
                pltpu.VMEM((lev + 1, 2, KXM), f32),
                pltpu.VMEM((lev + 1, 2, KXM), f32),
                dma((8,)),
                dma((2,)),
                dma((2,)),
                dma((2, wide)),
                dma((2, wide)),
                dma((lev,)),
                dma((lev,)),
            ],
            compiler_params=pltpu.CompilerParams(
                collective_id=0, has_side_effects=True, vmem_limit_bytes=56 * 2**20
            ),
            cost_estimate=pl.CostEstimate(
                flops=2 * 4 * levels * NXG * 2 * KXM,
                bytes_accessed=NXG * 2 * KXM * 2 + 4 * rows * chunk * 2,
                transcendentals=0,
            ),
        )(nonlinear.reshape(3, 2, rows, chunk), jnp.asarray(tables))
        pressure = pl.pallas_call(
            hand_over, out_shape=jax.ShapeDtypeStruct(pressure.shape, f32)
        )(pressure)
        return pressure.reshape(2, levels, 1, KXM)

    placed = (P(None, None, "lev", None, "wide"),)
    return jax.shard_map(
        local, mesh=mesh, in_specs=placed, out_specs=P(None, "lev", "wide", None), check_vma=False
    )
```

profile of v0, /device:TPU:17, one launch (start us, length us, event | category | flops | bytes accessed | tf_op | source)
XLA Modules:
  0.0 61.2 jit_solution(12730390730778042648)
XLA Ops:
  0.0 59.2 %shard_map.28.x_ref = f32[1536,128]{1,0:T(8,128)} custom-call(bf16[3,2,512,512]{3,2,1,0:T(8,128)(2,1)} %bitcast.2, bf16[4096,3072]{1,0:T(8,128)(2,1)} %constant.2.clone.tab_ref), custom_call_target="tpu_custom_call" | custom-call | flops 6442450944 | bytes 27262976 | tf_op jit(solution)/shard_map/pallas_call | solution.py:362
  59.2 2.1 %shard_map.29 = f32[1536,128]{1,0:T(8,128)} custom-call(f32[1536,128]{1,0:T(8,128)} %shard_map.28.x_ref), custom_call_target="tpu_custom_call" | custom-call | tf_op jit(solution)/shard_map/pallas_call | solution.py:403
where the time goes:
time: 61.9 us; the launch traced here: 61.2 us
  Pallas kernels  61.2 us (99%)
    pallas_call x1, Pallas kernels, local(): pl.pallas_call(functools.partial(kernel, wide, lev, rows_ky, levels), out...  59.2 us
    pallas_call x1, Pallas kernels, local(): pl.pallas_call(hand_over, out_shape=jax.ShapeDtypeStruct(pressure.shape,...  2.06 us

commit v1 on v0

v1 whole, which is shorter than its diff:
```python
import functools
import math

import jax
import jax.numpy as jnp
import ml_dtypes
import numpy as np
from jax import lax
from jax.experimental import pallas as pl
from jax.experimental.pallas import tpu as pltpu
from jax.sharding import PartitionSpec as P

NXG = 4096
KXM = 1536
MESH = pl.DeviceIdType.MESH
SEC = 512
TILE = 256
SECTIONS = KXM // SEC
PER = SEC // 128
DEEP = 2 * PER


def make_tables():
    places = np.arange(NXG, dtype=np.int32)
    waves = np.arange(KXM, dtype=np.int32) - KXM // 2
    phases = np.mod(places[:, None] * waves[None, :], NXG)
    turn = np.arange(NXG, dtype=np.float32) * np.float32(2.0 * math.pi / NXG)
    cosine = np.cos(turn).astype(ml_dtypes.bfloat16)[phases]
    sine = np.sin(turn).astype(ml_dtypes.bfloat16)[phases]
    return np.concatenate([cosine, sine], axis=1)


def level_rows(i, count=1):
    return pl.ds(pl.multiple_of(i * DEEP, DEEP), count * DEEP)


def kernel(
    wide, lev, rows_ky, levels,
    x_ref, tab_ref, out_ref,
    tab, send, recv, halo_lo, halo_hi, zpad, part, flow_out, flow_in, coef, from_lo,
    ends, last_val, first_val,
    tab_sem, halo_send, halo_recv, send_sem, recv_sem, flow_send, flow_recv, end_send, end_recv,
):
    f32, bf16 = jnp.float32, jnp.bfloat16
    chunk = x_ref.shape[3]
    line_rows = levels * rows_ky
    half = 2 * levels
    group_levels = max(16, 256 // rows_ky)
    group_rows = group_levels * rows_ky
    groups = levels // group_levels
    halo_rows = halo_lo.shape[1]
    spacing = 2.0 * math.pi / NXG
    me = lax.axis_index("wide")
    block = lax.axis_index("lev")
    chain = wide // 2
    q, h = me // 2, me % 2
    pair = me + 1 - 2 * h

    tab_parts = tab_sem.shape[1]
    tab_rows = chunk // tab_parts

    def tab_copy(side, i):
        owner = me if side == 0 else pair
        at = pl.multiple_of(owner * chunk + i * tab_rows, tab_rows)
        return pltpu.make_async_copy(
            tab_ref.at[pl.ds(at, tab_rows)],
            tab.at[pl.ds(side * chunk + i * tab_rows, tab_rows)],
            tab_sem.at[side, i],
        )

    barrier = pltpu.get_barrier_semaphore()
    pl.semaphore_signal(barrier, inc=1, device_id={"wide": pair}, device_id_type=MESH)

    @pl.when(q > 0)
    def _():
        pl.semaphore_signal(barrier, inc=1, device_id={"wide": me - 2}, device_id_type=MESH)

    @pl.when(q < chain - 1)
    def _():
        pl.semaphore_signal(barrier, inc=1, device_id={"wide": me + 2}, device_id_type=MESH)

    for step in range(1, lev):
        pl.semaphore_signal(
            barrier, inc=1, device_id={"lev": (block + step) % lev}, device_id_type=MESH
        )
    for side in range(2):
        for i in range(tab_parts):
            tab_copy(side, i).start()

    out_row = lax.broadcasted_iota(jnp.int32, (group_rows, group_rows), 0)
    in_row = lax.broadcasted_iota(jnp.int32, (group_rows, group_rows), 1)
    wanted = (out_row % group_levels) * rows_ky + out_row // group_levels
    shuffle = jnp.where(in_row == wanted, 1.0, 0.0).astype(bf16)

    def place(values, first):
        moved = jnp.dot(shuffle, values, preferred_element_type=f32).astype(bf16)
        for ky in range(rows_ky):
            send[ky, first:first + group_levels, :] = moved[
                ky * group_levels:(ky + 1) * group_levels
            ]

    upper_far = 1 - (2 * q) // chain
    far = upper_far * (chain - 1 - q) + (1 - upper_far) * q
    near_count = chain - 1 - far
    alone = far - near_count

    def unit(s):
        late = (s - alone + chain) // chain
        t = late * (s - alone)
        distance = (1 - late) * (far - s) + late * (near_count - t // 2)
        up = (1 - late) * upper_far + late * ((1 - upper_far) * (1 - t % 2) + upper_far * (t % 2))
        way = 2 * up - 1
        return q + way * distance, way

    def line_copy(d, which):
        rows = pl.ds(which * half, half)
        return pltpu.make_async_remote_copy(
            src_ref=send.at[2 * d + 1 - h, rows],
            dst_ref=recv.at[d, rows],
            send_sem=send_sem.at[which, d],
            recv_sem=recv_sem.at[which, d],
            device_id={"wide": pair},
            device_id_type=MESH,
        )

    for c in range(2):
        for g in range(groups):
            place(
                x_ref[0, c, g * group_rows:(g + 1) * group_rows, :],
                c * levels + g * group_levels,
            )
    has_prev = (q + chain - 1) // chain
    has_next = (2 * chain - 2 - q) // chain
    pl.semaphore_wait(barrier, lev + has_prev + has_next)

    to_prev = pltpu.make_async_remote_copy(
        src_ref=x_ref.at[2, :, 0:halo_rows],
        dst_ref=halo_hi,
        send_sem=halo_send.at[0],
        recv_sem=halo_recv.at[0],
        device_id={"lev": (block + lev - 1) % lev},
        device_id_type=MESH,
    )
    to_next = pltpu.make_async_remote_copy(
        src_ref=x_ref.at[2, :, line_rows - halo_rows:line_rows],
        dst_ref=halo_lo,
        send_sem=halo_send.at[1],
        recv_sem=halo_recv.at[1],
        device_id={"lev": (block + 1) % lev},
        device_id_type=MESH,
    )
    to_prev.start()
    to_next.start()
    first_unit, _ = unit(0)
    line_copy(first_unit, 0).start()

    for c in range(2):
        zpad[c, rows_ky:rows_ky + line_rows, :] = x_ref[2, c].astype(f32)
    to_prev.wait_recv()
    to_next.wait_recv()
    for c in range(2):
        low = halo_lo[c].astype(f32)[halo_rows - rows_ky:]
        high = halo_hi[c].astype(f32)[:rows_ky]
        zpad[c, 0:rows_ky, :] = jnp.where(block > 0, low, 0.0)
        zpad[c, rows_ky + line_rows:, :] = jnp.where(block < lev - 1, high, 0.0)
    ky_row = lax.broadcasted_iota(jnp.int32, (group_rows, chunk), 0) % rows_ky
    ky_scaled = ky_row.astype(f32) * spacing
    for c in range(2):
        for g in range(groups):
            at = g * group_rows
            upper = zpad[c, at + 2 * rows_ky:at + 2 * rows_ky + group_rows, :]
            lower = zpad[c, at:at + group_rows, :]
            turned = ky_scaled * x_ref[1, 1 - c, at:at + group_rows, :].astype(f32)
            slope = (upper - lower) * 0.5
            mixed = slope - turned if c == 0 else slope + turned
            place(mixed.astype(bf16), half + c * levels + g * group_levels)
    line_copy(first_unit, 1).start()

    def send_lines(s, carry):
        d, _ = unit(s)
        line_copy(d, 0).start()
        line_copy(d, 1).start()
        return carry

    lax.fori_loop(1, chain, send_lines, 0)

    def clear(slot):
        for k in range(SECTIONS):
            flow_in[slot, k] = jnp.zeros(flow_in.shape[2:], bf16)

    @pl.when(q == 0)
    def _():
        @pl.loop(0, chain)
        def _(slot):
            clear(slot)

    @pl.when(q == chain - 1)
    def _():
        @pl.loop(0, chain - 1)
        def _(slot):
            clear(slot)

        clear(chain)

    part_row = lax.broadcasted_iota(jnp.int32, (DEEP, 128), 0)
    lane = lax.broadcasted_iota(jnp.int32, (DEEP, 128), 1)

    def diagonal(ky, k):
        column = k * SEC + (part_row % PER) * 128 + lane
        kx = (column - KXM // 2).astype(f32) * spacing
        kyd = ky.astype(f32) * spacing
        return 2.0 + (kyd * kyd + kx * kx)

    own_diagonal = [diagonal(me, k) for k in range(SECTIONS)]

    def coef_step(i, carry):
        after = []
        for k in range(SECTIONS):
            shift, gain = carry[2 * k], carry[2 * k + 1]
            inverse = 1.0 / (own_diagonal[k] - shift)
            gain = gain * inverse
            coef[k, level_rows(i), :] = inverse
            from_lo[k, level_rows(i), :] = gain
            after += [inverse, gain]
        return tuple(after)

    zeros = jnp.zeros((DEEP, 128), f32)
    ones = jnp.ones((DEEP, 128), f32)
    lax.fori_loop(0, levels, coef_step, (zeros, ones) * SECTIONS)

    def unit_step(j, carry):
        i = levels - 1 - j
        after = []
        for k in range(SECTIONS):
            low = from_lo[k, level_rows(i), :] + coef[k, level_rows(i), :] * carry[k]
            from_lo[k, level_rows(i), :] = low
            after.append(low)
        return tuple(after)

    lax.fori_loop(0, levels, unit_step, (zeros,) * SECTIONS)

    for side in range(2):
        for i in range(tab_parts):
            tab_copy(side, i).wait()

    norm_scale = 1.0 / math.sqrt(NXG)

    def transform(d, k):
        lines = jnp.concatenate([send[2 * d + h], recv[d]], axis=1)
        for t in range(SEC // TILE):
            first = k * SEC + t * TILE
            with_cos = jnp.dot(lines, tab[:, first:first + TILE], preferred_element_type=f32)
            with_sin = jnp.dot(
                lines, tab[:, KXM + first:KXM + first + TILE], preferred_element_type=f32
            )
            kx = (
                lax.broadcasted_iota(jnp.int32, (1, TILE), 1) + first - KXM // 2
            ).astype(f32) * spacing
            n = levels
            fx_real = (with_cos[0:n] + with_sin[n:2 * n]) * norm_scale
            fx_imag = (with_cos[n:2 * n] - with_sin[0:n]) * norm_scale
            fg_real = (with_cos[2 * n:3 * n] + with_sin[3 * n:4 * n]) * norm_scale
            fg_imag = (with_cos[3 * n:4 * n] - with_sin[2 * n:3 * n]) * norm_scale
            source_real = kx * fx_imag - fg_real
            source_imag = -kx * fx_real - fg_imag
            for j in range(TILE // 128):
                at = slice(j * 128, (j + 1) * 128)
                row = t * (TILE // 128) + j
                part[k, pl.ds(row, n, stride=DEEP), :] = source_real[:, at]
                part[k, pl.ds(PER + row, n, stride=DEEP), :] = source_imag[:, at]

    def flow_copy(d, way, k):
        slot = jnp.where(q + way == d, jnp.where(way > 0, d, chain), d)
        return pltpu.make_async_remote_copy(
            src_ref=flow_out.at[d, k],
            dst_ref=flow_in.at[slot, k],
            send_sem=flow_send.at[d, k],
            recv_sem=flow_recv.at[slot, k],
            device_id={"wide": me + 2 * way},
            device_id_type=MESH,
        )

    def arrival(slot, k):
        return pltpu.make_async_remote_copy(
            src_ref=flow_out.at[0, k],
            dst_ref=flow_in.at[slot, k],
            send_sem=flow_send.at[0, k],
            recv_sem=flow_recv.at[slot, k],
            device_id={"wide": pair},
            device_id_type=MESH,
        )

    pairs = levels // 2
    step_pairs = 6
    loose = (pairs - 1) % step_pairs

    def rounded(value):
        return value.astype(bf16).astype(f32)

    def shape_noise(d, k):
        diag = diagonal(2 * d + h, k)
        root = 0.5 * (diag - jnp.sqrt(jnp.maximum(diag * diag - 4.0, 0.0)))
        once, twice = 2.0 * root, root * root

        def one_pair(i, carry):
            lost, older = carry
            rows = level_rows(2 * i, 2)
            both = part[k, rows, :] + flow_in[d, k, rows, :].astype(f32)
            value = both[:DEEP] + (once * lost - twice * older)
            low = rounded(value)
            lost, older = value - low, lost
            value = both[DEEP:] + (once * lost - twice * older)
            high = rounded(value)
            lost, older = value - high, lost
            flow_out[d, k, rows, :] = jnp.concatenate([low, high], axis=0).astype(bf16)
            return lost, older

        carry = (zeros, zeros)
        for i in range(loose):
            carry = one_pair(i, carry)

        def some_pairs(j, carry):
            for i in range(step_pairs):
                carry = one_pair(loose + j * step_pairs + i, carry)
            return carry

        lost, older = lax.fori_loop(0, (pairs - 1) // step_pairs, some_pairs, carry)
        rows, rest = pl.ds((levels - 2) * DEEP, 2 * DEEP), pl.ds(levels * DEEP, 2 * DEEP)
        both = part[k, rows, :] + flow_in[d, k, rows, :].astype(f32)
        both = both + flow_in[d, k, rest, :].astype(f32)
        both = both + jnp.concatenate([once * lost - twice * older, -(twice * lost)], axis=0)
        kept = rounded(both)
        flow_out[d, k, rows, :] = kept.astype(bf16)
        flow_out[d, k, rest, :] = (both - kept).astype(bf16)

    def pass_on(s, carry):
        d, way = unit(s)
        line_copy(d, 0).wait_recv()
        line_copy(d, 1).wait_recv()
        before = q - way
        for k in range(SECTIONS):
            transform(d, k)

            @pl.when(jnp.logical_and(before >= 0, before < chain))
            def _():
                arrival(d, k).wait_recv()

            shape_noise(d, k)
            flow_copy(d, way, k).start()
        return carry

    lax.fori_loop(0, chain - 1, pass_on, 0)

    line_copy(q, 0).wait_recv()
    line_copy(q, 1).wait_recv()
    for k in range(SECTIONS):
        transform(q, k)

    def end_copy(step, slot, k):
        return pltpu.make_async_remote_copy(
            src_ref=ends.at[slot, k],
            dst_ref=ends.at[slot, k],
            send_sem=end_send.at[step, k],
            recv_sem=end_recv.at[step, k],
            device_id={"lev": (block + step) % lev},
            device_id_type=MESH,
        )

    for k in range(SECTIONS):
        @pl.when(q > 0)
        def _():
            arrival(q, k).wait_recv()

        @pl.when(q < chain - 1)
        def _():
            arrival(chain, k).wait_recv()

        for rest_at, rows_at in ((levels * DEEP, (levels - 2) * DEEP),):
            rows, rest = pl.ds(rows_at, 2 * DEEP), pl.ds(rest_at, 2 * DEEP)
            part[k, rows, :] = part[k, rows, :] + (
                flow_in[q, k, rest, :].astype(f32) + flow_in[chain, k, rest, :].astype(f32)
            )

        def down_pair(i, carry):
            value, first = carry
            rows = level_rows(2 * i, 2)
            both = part[k, rows, :] + (
                flow_in[q, k, rows, :].astype(f32) + flow_in[chain, k, rows, :].astype(f32)
            )
            weighted = from_lo[k, rows, :] * both
            first = first + (weighted[:DEEP] + weighted[DEEP:])
            inverse = coef[k, rows, :]
            low = (both[:DEEP] + value) * inverse[:DEEP]
            high = (both[DEEP:] + low) * inverse[DEEP:]
            part[k, rows, :] = jnp.concatenate([low, high], axis=0)
            return high, first

        value, first = lax.fori_loop(0, pairs, down_pair, (zeros, zeros), unroll=8)
        ends[block, k, 0:DEEP, :] = first
        ends[block, k, DEEP:2 * DEEP, :] = value
        for step in range(1, lev):
            end_copy(step, block, k).start()

    for k in range(SECTIONS):
        near = from_lo[k, 0:DEEP, :]
        distant = from_lo[k, (levels - 1) * DEEP:levels * DEEP, :]
        ratio = near
        ratios, inverses, leads = [ratio], [None], [None]
        for b in range(1, lev):
            inverse = 1.0 / (1.0 - near * ratio)
            lead = distant * ratio * inverse
            ratio = near + lead * distant
            ratios.append(ratio)
            inverses.append(inverse)
            leads.append(lead)
        for step in range(1, lev):
            end_copy(step, (block + lev - step) % lev, k).wait_recv()
        value = ends[0, k, DEEP:2 * DEEP, :]
        values = [value]
        for b in range(1, lev):
            first = ends[b, k, 0:DEEP, :] + near * value
            value = ends[b, k, DEEP:2 * DEEP, :] + distant * value + leads[b] * first
            values.append(value)
        follow = zeros
        first_val[lev] = follow
        last_val[0] = follow
        for b in range(lev - 1, 0, -1):
            follow = inverses[b] * (
                ends[b, k, 0:DEEP, :] + near * values[b - 1] + distant * follow
            )
            first_val[b] = follow
            last_val[b] = values[b - 1] + ratios[b - 1] * follow
        below = last_val[block]

        def up_step(j, carry):
            rows = level_rows(levels - 1 - j)
            carry = part[k, rows, :] + coef[k, rows, :] * carry
            part[k, rows, :] = carry + from_lo[k, rows, :] * below
            return carry

        lax.fori_loop(0, levels, up_step, first_val[block + 1], unroll=8)
        tiles = KXM // 128
        for c in range(2):
            for j in range(PER):
                out_ref[pl.ds(c * levels * tiles + k * PER + j, levels, stride=tiles), :] = part[
                    k, pl.ds(c * PER + j, levels, stride=DEEP), :
                ]

    to_prev.wait_send()
    to_next.wait_send()

    def lines_sent(d, carry):
        line_copy(d, 0).wait_send()
        line_copy(d, 1).wait_send()
        return carry

    lax.fori_loop(0, chain, lines_sent, 0)

    def flows_sent(s, carry):
        d, way = unit(s)
        for k in range(SECTIONS):
            flow_copy(d, way, k).wait_send()
        return carry

    lax.fori_loop(0, chain - 1, flows_sent, 0)
    for k in range(SECTIONS):
        for step in range(1, lev):
            end_copy(step, block, k).wait_send()


def hand_over(x_ref, out_ref):
    out_ref[...] = x_ref[...]


def solution(mesh):
    wide, lev = mesh.shape["wide"], mesh.shape["lev"]
    tables = make_tables()

    def local(nonlinear):
        _, _, levels, rows_ky, chunk = nonlinear.shape
        rows = levels * rows_ky
        halo_rows = max(16, rows_ky)
        chain = wide // 2
        f32, bf16 = jnp.float32, jnp.bfloat16
        dma = pltpu.SemaphoreType.DMA
        pressure = pl.pallas_call(
            functools.partial(kernel, wide, lev, rows_ky, levels),
            out_shape=jax.ShapeDtypeStruct((2 * levels * KXM // 128, 128), f32),
            in_specs=[
                pl.BlockSpec(memory_space=pltpu.VMEM),
                pl.BlockSpec(memory_space=pl.ANY),
            ],
            out_specs=pl.BlockSpec(memory_space=pltpu.VMEM),
            scratch_shapes=[
                pltpu.VMEM((2 * chunk, 2 * KXM), bf16),
                pltpu.VMEM((rows_ky, 4 * levels, chunk), bf16),
                pltpu.VMEM((chain, 4 * levels, chunk), bf16),
                pltpu.VMEM((2, halo_rows, chunk), bf16),
                pltpu.VMEM((2, halo_rows, chunk), bf16),
                pltpu.VMEM((2, rows + 2 * rows_ky, chunk), f32),
                pltpu.VMEM((SECTIONS, levels * DEEP, 128), f32),
                pltpu.VMEM((chain, SECTIONS, (levels + 2) * DEEP, 128), bf16),
                pltpu.VMEM((chain + 1, SECTIONS, (levels + 2) * DEEP, 128), bf16),
                pltpu.VMEM((SECTIONS, levels * DEEP, 128), f32),
                pltpu.VMEM((SECTIONS, levels * DEEP, 128), f32),
                pltpu.VMEM((lev, SECTIONS, 2 * DEEP, 128), f32),
                pltpu.VMEM((lev + 1, DEEP, 128), f32),
                pltpu.VMEM((lev + 1, DEEP, 128), f32),
                dma((2, 4)),
                dma((2,)),
                dma((2,)),
                dma((2, chain)),
                dma((2, chain)),
                dma((chain, SECTIONS)),
                dma((chain + 1, SECTIONS)),
                dma((lev, SECTIONS)),
                dma((lev, SECTIONS)),
            ],
            compiler_params=pltpu.CompilerParams(
                collective_id=0, has_side_effects=True, vmem_limit_bytes=56 * 2**20
            ),
            cost_estimate=pl.CostEstimate(
                flops=2 * 4 * levels * NXG * 2 * KXM,
                bytes_accessed=2 * chunk * 2 * KXM * 2 + 4 * rows * chunk * 2,
                transcendentals=0,
            ),
        )(nonlinear.reshape(3, 2, rows, chunk), jnp.asarray(tables))
        pressure = pl.pallas_call(
            hand_over, out_shape=jax.ShapeDtypeStruct(pressure.shape, f32)
        )(pressure)
        return pressure.reshape(2, levels, 1, KXM)

    placed = (P(None, None, "lev", None, "wide"),)
    return jax.shard_map(
        local, mesh=mesh, in_specs=placed, out_specs=P(None, "lev", "wide", None), check_vma=False
    )
```

time: 61.9 us -> 49.6 us (0.80)
  Pallas kernels: 61.2 us -> 49.4 us
    pallas_call x1, Pallas kernels: 59.2 us -> 47.3 us  [local(): pl.pallas_call(functools.partial(kernel, wide, lev, rows_ky, levels), out...]
where the time goes in v1:
time: 49.6 us; the launch traced here: 49.4 us
  Pallas kernels  49.4 us (100%)
    pallas_call x1, Pallas kernels, local(): pl.pallas_call(functools.partial(kernel, wide, lev, rows_ky, levels), out...  47.3 us
    pallas_call x1, Pallas kernels, local(): pl.pallas_call(hand_over, out_shape=jax.ShapeDtypeStruct(pressure.shape,...  2.06 us

profile of v1, /device:TPU:17, one launch (start us, length us, event | category | flops | bytes accessed | tf_op | source)
XLA Modules:
  0.0 49.4 jit_solution(8395323040018045867)
XLA Ops:
  0.0 47.3 %shard_map.28.x_ref = f32[1536,128]{1,0:T(8,128)} custom-call(bf16[3,2,512,512]{3,2,1,0:T(8,128)(2,1)} %bitcast.2, bf16[4096,3072]{1,0:T(8,128)(2,1)} %constant.2.clone.tab_ref), custom_call_target="tpu_custom_call" | custom-call | flops 6442450944 | bytes 8388608 | tf_op jit(solution)/shard_map/pallas_call | solution.py:486
  47.3 2.1 %shard_map.29 = f32[1536,128]{1,0:T(8,128)} custom-call(f32[1536,128]{1,0:T(8,128)} %shard_map.28.x_ref), custom_call_target="tpu_custom_call" | custom-call | tf_op jit(solution)/shard_map/pallas_call | solution.py:528

commit v2 on v1

--- a/solution.py
+++ b/solution.py
@@ -37,14 +37,14 @@
 def kernel(
     wide, lev, rows_ky, levels,
     x_ref, tab_ref, out_ref,
-    tab, send, recv, halo_lo, halo_hi, zpad, part, flow_out, flow_in, coef, from_lo,
-    ends, last_val, first_val,
-    tab_sem, halo_send, halo_recv, send_sem, recv_sem, flow_send, flow_recv, end_send, end_recv,
+    x_buf, tab, send, recv, halo_lo, halo_hi, zpad, part, flow_out, flow_in, coef, from_lo,
+    ends, last_val, first_val, lost_val,
+    x_sem, tab_sem, halo_send, halo_recv, send_sem, recv_sem, flow_send, flow_recv, end_send, end_recv,
 ):
     f32, bf16 = jnp.float32, jnp.bfloat16
     chunk = x_ref.shape[3]
     line_rows = levels * rows_ky
-    half = 2 * levels
+    half_levels = levels // 2
     group_levels = max(16, 256 // rows_ky)
     group_rows = group_levels * rows_ky
     groups = levels // group_levels
@@ -83,6 +83,12 @@
         pl.semaphore_signal(
             barrier, inc=1, device_id={"lev": (block + step) % lev}, device_id_type=MESH
         )
+    def x_copy(term, c):
+        return pltpu.make_async_copy(x_ref.at[term, c], x_buf.at[term, c], x_sem.at[term, c])
+
+    for term in (0, 2, 1):
+        for c in range(2):
+            x_copy(term, c).start()
     for side in range(2):
         for i in range(tab_parts):
             tab_copy(side, i).start()
@@ -92,10 +98,10 @@
     wanted = (out_row % group_levels) * rows_ky + out_row // group_levels
     shuffle = jnp.where(in_row == wanted, 1.0, 0.0).astype(bf16)
 
-    def place(values, first):
+    def place(values, c, g):
         moved = jnp.dot(shuffle, values, preferred_element_type=f32).astype(bf16)
         for ky in range(rows_ky):
-            send[ky, first:first + group_levels, :] = moved[
+            send[ky, c, g * group_levels:(g + 1) * group_levels, :] = moved[
                 ky * group_levels:(ky + 1) * group_levels
             ]
 
@@ -112,27 +118,20 @@
         way = 2 * up - 1
         return q + way * distance, way
 
-    def line_copy(d, which):
-        rows = pl.ds(which * half, half)
+    def line_copy(d, which, g):
+        rows = (pl.ds(2 * which, 2), pl.ds(g * half_levels, half_levels))
         return pltpu.make_async_remote_copy(
-            src_ref=send.at[2 * d + 1 - h, rows],
-            dst_ref=recv.at[d, rows],
-            send_sem=send_sem.at[which, d],
-            recv_sem=recv_sem.at[which, d],
+            src_ref=send.at[(2 * d + 1 - h,) + rows],
+            dst_ref=recv.at[(d,) + rows],
+            send_sem=send_sem.at[which, g, d],
+            recv_sem=recv_sem.at[which, g, d],
             device_id={"wide": pair},
             device_id_type=MESH,
         )
 
-    for c in range(2):
-        for g in range(groups):
-            place(
-                x_ref[0, c, g * group_rows:(g + 1) * group_rows, :],
-                c * levels + g * group_levels,
-            )
     has_prev = (q + chain - 1) // chain
     has_next = (2 * chain - 2 - q) // chain
     pl.semaphore_wait(barrier, lev + has_prev + has_next)
-
     to_prev = pltpu.make_async_remote_copy(
         src_ref=x_ref.at[2, :, 0:halo_rows],
         dst_ref=halo_hi,
@@ -149,37 +148,54 @@
         device_id={"lev": (block + 1) % lev},
         device_id_type=MESH,
     )
+    to_next.start()
     to_prev.start()
-    to_next.start()
-    first_unit, _ = unit(0)
-    line_copy(first_unit, 0).start()
-
+    first_unit, first_way = unit(0)
     for c in range(2):
-        zpad[c, rows_ky:rows_ky + line_rows, :] = x_ref[2, c].astype(f32)
-    to_prev.wait_recv()
-    to_next.wait_recv()
+        x_copy(0, c).wait()
+    for part_of in range(2):
+        for g in range(part_of * groups // 2, (part_of + 1) * groups // 2):
+            for c in range(2):
+                place(x_buf[0, c, g * group_rows:(g + 1) * group_rows, :], c, g)
+        if part_of == 0:
+            line_copy(first_unit, 0, 0).start()
+
     for c in range(2):
-        low = halo_lo[c].astype(f32)[halo_rows - rows_ky:]
-        high = halo_hi[c].astype(f32)[:rows_ky]
-        zpad[c, 0:rows_ky, :] = jnp.where(block > 0, low, 0.0)
-        zpad[c, rows_ky + line_rows:, :] = jnp.where(block < lev - 1, high, 0.0)
+        x_copy(2, c).wait()
+        zpad[c, rows_ky:rows_ky + line_rows, :] = x_buf[2, c].astype(f32)
+    for c in range(2):
+        x_copy(1, c).wait()
     ky_row = lax.broadcasted_iota(jnp.int32, (group_rows, chunk), 0) % rows_ky
     ky_scaled = ky_row.astype(f32) * spacing
-    for c in range(2):
-        for g in range(groups):
-            at = g * group_rows
-            upper = zpad[c, at + 2 * rows_ky:at + 2 * rows_ky + group_rows, :]
-            lower = zpad[c, at:at + group_rows, :]
-            turned = ky_scaled * x_ref[1, 1 - c, at:at + group_rows, :].astype(f32)
-            slope = (upper - lower) * 0.5
-            mixed = slope - turned if c == 0 else slope + turned
-            place(mixed.astype(bf16), half + c * levels + g * group_levels)
-    line_copy(first_unit, 1).start()
+    for part_of in range(2):
+        if part_of == 0:
+            to_next.wait_recv()
+            for c in range(2):
+                low = halo_lo[c].astype(f32)[halo_rows - rows_ky:]
+                zpad[c, 0:rows_ky, :] = jnp.where(block > 0, low, 0.0)
+        else:
+            to_prev.wait_recv()
+            for c in range(2):
+                high = halo_hi[c].astype(f32)[:rows_ky]
+                zpad[c, rows_ky + line_rows:, :] = jnp.where(block < lev - 1, high, 0.0)
+        for g in range(part_of * groups // 2, (part_of + 1) * groups // 2):
+            for c in range(2):
+                at = g * group_rows
+                upper = zpad[c, at + 2 * rows_ky:at + 2 * rows_ky + group_rows, :]
+                lower = zpad[c, at:at + group_rows, :]
+                turned = ky_scaled * x_buf[1, 1 - c, at:at + group_rows, :].astype(f32)
+                slope = (upper - lower) * 0.5
+                mixed = slope - turned if c == 0 else slope + turned
+                place(mixed.astype(bf16), 2 + c, g)
+        line_copy(first_unit, 1, part_of).start()
+        if part_of == 0:
+            line_copy(first_unit, 0, 1).start()
 
     def send_lines(s, carry):
         d, _ = unit(s)
-        line_copy(d, 0).start()
-        line_copy(d, 1).start()
+        for which in range(2):
+            for g in range(2):
+                line_copy(d, which, g).start()
         return carry
 
     lax.fori_loop(1, chain, send_lines, 0)
@@ -245,8 +261,15 @@
 
     norm_scale = 1.0 / math.sqrt(NXG)
 
-    def transform(d, k):
-        lines = jnp.concatenate([send[2 * d + h], recv[d]], axis=1)
+    def transform(d, k, begin, n):
+        rows = slice(begin, begin + n)
+        lines = jnp.concatenate(
+            [
+                send[2 * d + h, :, rows, :].reshape(4 * n, chunk),
+                recv[d, :, rows, :].reshape(4 * n, chunk),
+            ],
+            axis=1,
+        )
         for t in range(SEC // TILE):
             first = k * SEC + t * TILE
             with_cos = jnp.dot(lines, tab[:, first:first + TILE], preferred_element_type=f32)
@@ -256,7 +279,6 @@
             kx = (
                 lax.broadcasted_iota(jnp.int32, (1, TILE), 1) + first - KXM // 2
             ).astype(f32) * spacing
-            n = levels
             fx_real = (with_cos[0:n] + with_sin[n:2 * n]) * norm_scale
             fx_imag = (with_cos[n:2 * n] - with_sin[0:n]) * norm_scale
             fg_real = (with_cos[2 * n:3 * n] + with_sin[3 * n:4 * n]) * norm_scale
@@ -265,39 +287,49 @@
             source_imag = -kx * fx_real - fg_imag
             for j in range(TILE // 128):
                 at = slice(j * 128, (j + 1) * 128)
-                row = t * (TILE // 128) + j
+                row = begin * DEEP + t * (TILE // 128) + j
                 part[k, pl.ds(row, n, stride=DEEP), :] = source_real[:, at]
                 part[k, pl.ds(PER + row, n, stride=DEEP), :] = source_imag[:, at]
 
-    def flow_copy(d, way, k):
+    flow_rows = (pl.ds(0, half_levels * DEEP), pl.ds(half_levels * DEEP, (half_levels + 2) * DEEP))
+
+    def flow_copy(d, way, k, g):
         slot = jnp.where(q + way == d, jnp.where(way > 0, d, chain), d)
         return pltpu.make_async_remote_copy(
-            src_ref=flow_out.at[d, k],
-            dst_ref=flow_in.at[slot, k],
-            send_sem=flow_send.at[d, k],
-            recv_sem=flow_recv.at[slot, k],
+            src_ref=flow_out.at[d, k, flow_rows[g]],
+            dst_ref=flow_in.at[slot, k, flow_rows[g]],
+            send_sem=flow_send.at[d, k, g],
+            recv_sem=flow_recv.at[slot, k, g],
             device_id={"wide": me + 2 * way},
             device_id_type=MESH,
         )
 
-    def arrival(slot, k):
+    def arrival(slot, k, g):
         return pltpu.make_async_remote_copy(
-            src_ref=flow_out.at[0, k],
-            dst_ref=flow_in.at[slot, k],
-            send_sem=flow_send.at[0, k],
-            recv_sem=flow_recv.at[slot, k],
+            src_ref=flow_out.at[0, k, flow_rows[g]],
+            dst_ref=flow_in.at[slot, k, flow_rows[g]],
+            send_sem=flow_send.at[0, k, g],
+            recv_sem=flow_recv.at[slot, k, g],
             device_id={"wide": pair},
             device_id_type=MESH,
         )
 
-    pairs = levels // 2
-    step_pairs = 6
-    loose = (pairs - 1) % step_pairs
+    def over_pairs(body, begin, count, carry):
+        group = max(n for n in range(1, 9) if count % n == 0)
+
+        def some(j, carry):
+            for i in range(group):
+                carry = body(begin + j * group + i, carry)
+            return carry
+
+        return lax.fori_loop(0, count // group, some, carry)
+
+    half_pairs = half_levels // 2
 
     def rounded(value):
         return value.astype(bf16).astype(f32)
 
-    def shape_noise(d, k):
+    def shape_noise(d, k, g, carry):
         diag = diagonal(2 * d + h, k)
         root = 0.5 * (diag - jnp.sqrt(jnp.maximum(diag * diag - 4.0, 0.0)))
         once, twice = 2.0 * root, root * root
@@ -315,16 +347,9 @@
             flow_out[d, k, rows, :] = jnp.concatenate([low, high], axis=0).astype(bf16)
             return lost, older
 
-        carry = (zeros, zeros)
-        for i in range(loose):
-            carry = one_pair(i, carry)
-
-        def some_pairs(j, carry):
-            for i in range(step_pairs):
-                carry = one_pair(loose + j * step_pairs + i, carry)
-            return carry
-
-        lost, older = lax.fori_loop(0, (pairs - 1) // step_pairs, some_pairs, carry)
+        if g == 0:
+            return over_pairs(one_pair, 0, half_pairs, carry)
+        lost, older = over_pairs(one_pair, half_pairs, half_pairs - 1, carry)
         rows, rest = pl.ds((levels - 2) * DEEP, 2 * DEEP), pl.ds(levels * DEEP, 2 * DEEP)
         both = part[k, rows, :] + flow_in[d, k, rows, :].astype(f32)
         both = both + flow_in[d, k, rest, :].astype(f32)
@@ -332,29 +357,51 @@
         kept = rounded(both)
         flow_out[d, k, rows, :] = kept.astype(bf16)
         flow_out[d, k, rest, :] = (both - kept).astype(bf16)
+        return carry
+
+    def await_flow(d, way, k, g):
+        before = q - way
+
+        @pl.when(jnp.logical_and(before >= 0, before < chain))
+        def _():
+            arrival(d, k, g).wait_recv()
+
+    def await_lines(d, g):
+        for which in range(2):
+            line_copy(d, which, g).wait_recv()
+
+    for g in range(2):
+        await_lines(first_unit, g)
+        for k in range(SECTIONS):
+            transform(first_unit, k, g * half_levels, half_levels)
+            await_flow(first_unit, first_way, k, g)
+            if g == 0:
+                lost, older = shape_noise(first_unit, k, g, (zeros, zeros))
+                lost_val[k, 0] = lost
+                lost_val[k, 1] = older
+            else:
+                shape_noise(first_unit, k, g, (lost_val[k, 0], lost_val[k, 1]))
+            flow_copy(first_unit, first_way, k, g).start()
 
     def pass_on(s, carry):
         d, way = unit(s)
-        line_copy(d, 0).wait_recv()
-        line_copy(d, 1).wait_recv()
-        before = q - way
+        await_lines(d, 0)
+        await_lines(d, 1)
         for k in range(SECTIONS):
-            transform(d, k)
-
-            @pl.when(jnp.logical_and(before >= 0, before < chain))
-            def _():
-                arrival(d, k).wait_recv()
-
-            shape_noise(d, k)
-            flow_copy(d, way, k).start()
+            transform(d, k, 0, levels)
+            lost = (zeros, zeros)
+            for g in range(2):
+                await_flow(d, way, k, g)
+                lost = shape_noise(d, k, g, lost)
+                flow_copy(d, way, k, g).start()
         return carry
 
-    lax.fori_loop(0, chain - 1, pass_on, 0)
-
-    line_copy(q, 0).wait_recv()
-    line_copy(q, 1).wait_recv()
+    lax.fori_loop(1, chain - 1, pass_on, 0)
+
+    await_lines(q, 0)
+    await_lines(q, 1)
     for k in range(SECTIONS):
-        transform(q, k)
+        transform(q, k, 0, levels)
 
     def end_copy(step, slot, k):
         return pltpu.make_async_remote_copy(
@@ -366,21 +413,7 @@
             device_id_type=MESH,
         )
 
-    for k in range(SECTIONS):
-        @pl.when(q > 0)
-        def _():
-            arrival(q, k).wait_recv()
-
-        @pl.when(q < chain - 1)
-        def _():
-            arrival(chain, k).wait_recv()
-
-        for rest_at, rows_at in ((levels * DEEP, (levels - 2) * DEEP),):
-            rows, rest = pl.ds(rows_at, 2 * DEEP), pl.ds(rest_at, 2 * DEEP)
-            part[k, rows, :] = part[k, rows, :] + (
-                flow_in[q, k, rest, :].astype(f32) + flow_in[chain, k, rest, :].astype(f32)
-            )
-
+    def down_pass(k):
         def down_pair(i, carry):
             value, first = carry
             rows = level_rows(2 * i, 2)
@@ -395,13 +428,29 @@
             part[k, rows, :] = jnp.concatenate([low, high], axis=0)
             return high, first
 
-        value, first = lax.fori_loop(0, pairs, down_pair, (zeros, zeros), unroll=8)
+        carry = (zeros, zeros)
+        for g in range(2):
+            @pl.when(q > 0)
+            def _():
+                arrival(q, k, g).wait_recv()
+
+            @pl.when(q < chain - 1)
+            def _():
+                arrival(chain, k, g).wait_recv()
+
+            if g == 1:
+                rows, rest = pl.ds((levels - 2) * DEEP, 2 * DEEP), pl.ds(levels * DEEP, 2 * DEEP)
+                part[k, rows, :] = part[k, rows, :] + (
+                    flow_in[q, k, rest, :].astype(f32) + flow_in[chain, k, rest, :].astype(f32)
+                )
+            carry = over_pairs(down_pair, g * half_pairs, half_pairs, carry)
+        value, first = carry
         ends[block, k, 0:DEEP, :] = first
         ends[block, k, DEEP:2 * DEEP, :] = value
         for step in range(1, lev):
             end_copy(step, block, k).start()
 
-    for k in range(SECTIONS):
+    def up_pass(k):
         near = from_lo[k, 0:DEEP, :]
         distant = from_lo[k, (levels - 1) * DEEP:levels * DEEP, :]
         ratio = near
@@ -432,13 +481,18 @@
             last_val[b] = values[b - 1] + ratios[b - 1] * follow
         below = last_val[block]
 
-        def up_step(j, carry):
-            rows = level_rows(levels - 1 - j)
-            carry = part[k, rows, :] + coef[k, rows, :] * carry
-            part[k, rows, :] = carry + from_lo[k, rows, :] * below
-            return carry
-
-        lax.fori_loop(0, levels, up_step, first_val[block + 1], unroll=8)
+        def up_pair(j, carry):
+            rows = level_rows(levels - 2 - 2 * j, 2)
+            both, inverse = part[k, rows, :], coef[k, rows, :]
+            high = both[DEEP:] + inverse[DEEP:] * carry
+            low = both[:DEEP] + inverse[:DEEP] * high
+            gain = from_lo[k, rows, :]
+            part[k, rows, :] = jnp.concatenate(
+                [low + gain[:DEEP] * below, high + gain[DEEP:] * below], axis=0
+            )
+            return low
+
+        over_pairs(up_pair, 0, levels // 2, first_val[block + 1])
         tiles = KXM // 128
         for c in range(2):
             for j in range(PER):
@@ -446,12 +500,20 @@
                     k, pl.ds(c * PER + j, levels, stride=DEEP), :
                 ]
 
+    for k in range(SECTIONS):
+        down_pass(k)
+        if k > 0 and k < SECTIONS - 1:
+            up_pass(k - 1)
+    for k in range(max(SECTIONS - 2, 0), SECTIONS):
+        up_pass(k)
+
     to_prev.wait_send()
     to_next.wait_send()
 
     def lines_sent(d, carry):
-        line_copy(d, 0).wait_send()
-        line_copy(d, 1).wait_send()
+        for which in range(2):
+            for g in range(2):
+                line_copy(d, which, g).wait_send()
         return carry
 
     lax.fori_loop(0, chain, lines_sent, 0)
@@ -459,17 +521,14 @@
     def flows_sent(s, carry):
         d, way = unit(s)
         for k in range(SECTIONS):
-            flow_copy(d, way, k).wait_send()
+            for g in range(2):
+                flow_copy(d, way, k, g).wait_send()
         return carry
 
     lax.fori_loop(0, chain - 1, flows_sent, 0)
     for k in range(SECTIONS):
         for step in range(1, lev):
             end_copy(step, block, k).wait_send()
-
-
-def hand_over(x_ref, out_ref):
-    out_ref[...] = x_ref[...]
 
 
 def solution(mesh):
@@ -485,16 +544,17 @@
         dma = pltpu.SemaphoreType.DMA
         pressure = pl.pallas_call(
             functools.partial(kernel, wide, lev, rows_ky, levels),
-            out_shape=jax.ShapeDtypeStruct((2 * levels * KXM // 128, 128), f32),
+            out_shape=pltpu.VMEM((2 * levels * KXM // 128, 128), f32),
             in_specs=[
-                pl.BlockSpec(memory_space=pltpu.VMEM),
+                pl.BlockSpec(memory_space=pl.ANY),
                 pl.BlockSpec(memory_space=pl.ANY),
             ],
             out_specs=pl.BlockSpec(memory_space=pltpu.VMEM),
             scratch_shapes=[
+                pltpu.VMEM((3, 2, rows, chunk), bf16),
                 pltpu.VMEM((2 * chunk, 2 * KXM), bf16),
-                pltpu.VMEM((rows_ky, 4 * levels, chunk), bf16),
-                pltpu.VMEM((chain, 4 * levels, chunk), bf16),
+                pltpu.VMEM((rows_ky, 4, levels, chunk), bf16),
+                pltpu.VMEM((chain, 4, levels, chunk), bf16),
                 pltpu.VMEM((2, halo_rows, chunk), bf16),
                 pltpu.VMEM((2, halo_rows, chunk), bf16),
                 pltpu.VMEM((2, rows + 2 * rows_ky, chunk), f32),
@@ -506,13 +566,15 @@
                 pltpu.VMEM((lev, SECTIONS, 2 * DEEP, 128), f32),
                 pltpu.VMEM((lev + 1, DEEP, 128), f32),
                 pltpu.VMEM((lev + 1, DEEP, 128), f32),
+                pltpu.VMEM((SECTIONS, 2, DEEP, 128), f32),
+                dma((3, 2)),
                 dma((2, 4)),
                 dma((2,)),
                 dma((2,)),
-                dma((2, chain)),
-                dma((2, chain)),
-                dma((chain, SECTIONS)),
-                dma((chain + 1, SECTIONS)),
+                dma((2, 2, chain)),
+                dma((2, 2, chain)),
+                dma((chain, SECTIONS, 2)),
+                dma((chain + 1, SECTIONS, 2)),
                 dma((lev, SECTIONS)),
                 dma((lev, SECTIONS)),
             ],
@@ -525,9 +587,6 @@
                 transcendentals=0,
             ),
         )(nonlinear.reshape(3, 2, rows, chunk), jnp.asarray(tables))
-        pressure = pl.pallas_call(
-            hand_over, out_shape=jax.ShapeDtypeStruct(pressure.shape, f32)
-        )(pressure)
         return pressure.reshape(2, levels, 1, KXM)
 
     placed = (P(None, None, "lev", None, "wide"),)

time: 49.6 us -> 42.3 us (0.85)
  Pallas kernels: 49.4 us -> 41.3 us
  local copies, waits for them, and re-layouts: 0 us -> 0.88 us
    pallas_call x1, Pallas kernels: 47.3 us -> 41.3 us  [local(): pl.pallas_call(functools.partial(kernel, wide, lev, rows_ky, levels), out...]
    pallas_call x1 -> x0, Pallas kernels: 2.06 us -> none  [local(): pl.pallas_call(hand_over, out_shape=jax.ShapeDtypeStruct(pressure.shape,...]
    unnamed x0 -> x1, local copies, waits for them, and re-layouts: none -> 0.88 us
where the time goes in v2:
time: 42.3 us; the launch traced here: 42.2 us
  Pallas kernels  41.3 us (98%)
  local copies, waits for them, and re-layouts  0.88 us (2%)
    pallas_call x1, Pallas kernels, local(): pl.pallas_call(functools.partial(kernel, wide, lev, rows_ky, levels), out...  41.3 us
    unnamed x1, local copies, waits for them, and re-layouts  0.88 us

profile of v2, /device:TPU:17, one launch (start us, length us, event | category | flops | bytes accessed | tf_op | source)
XLA Modules:
  0.0 42.2 jit_solution(6581559623628538572)
XLA Ops:
  0.0 41.3 %shard_map.28 = f32[1536,128]{1,0:T(8,128)S(1)} custom-call(bf16[3,2,512,512]{3,2,1,0:T(8,128)(2,1)} %bitcast.3, bf16[4096,3072]{1,0:T(8,128)(2,1)} %constant.2.clone.tab_ref), custom_call_target="tpu_custom_call" | custom-call | flops 6442450944 | bytes 8388608 | tf_op jit(solution)/shard_map/pallas_call | solution.py:545
  41.3 0.9 %copy.5 = f32[2,64,1,1536]{3,2,1,0:T(1,128)} copy(f32[2,64,1,1536]{3,2,1,0:T(1,128)S(1)} %bitcast.2) | data formatting | bytes 1572864

commit v3 on v2

--- a/solution.py
+++ b/solution.py
@@ -37,7 +37,7 @@
 def kernel(
     wide, lev, rows_ky, levels,
     x_ref, tab_ref, out_ref,
-    x_buf, tab, send, recv, halo_lo, halo_hi, zpad, part, flow_out, flow_in, coef, from_lo,
+    x_buf, tab, send, recv, halo_lo, halo_hi, zpad, part, own_part, flow_out, flow_in, coef, from_lo,
     ends, last_val, first_val, lost_val,
     x_sem, tab_sem, halo_send, halo_recv, send_sem, recv_sem, flow_send, flow_recv, end_send, end_recv,
 ):
@@ -55,13 +55,14 @@
     chain = wide // 2
     q, h = me // 2, me % 2
     pair = me + 1 - 2 * h
+    has_prev = (q + chain - 1) // chain
+    has_next = (2 * chain - 2 - q) // chain
 
     tab_parts = tab_sem.shape[1]
     tab_rows = chunk // tab_parts
 
     def tab_copy(side, i):
-        owner = me if side == 0 else pair
-        at = pl.multiple_of(owner * chunk + i * tab_rows, tab_rows)
+        at = pl.multiple_of((me if side == 0 else pair) * chunk + i * tab_rows, tab_rows)
         return pltpu.make_async_copy(
             tab_ref.at[pl.ds(at, tab_rows)],
             tab.at[pl.ds(side * chunk + i * tab_rows, tab_rows)],
@@ -89,10 +90,6 @@
     for term in (0, 2, 1):
         for c in range(2):
             x_copy(term, c).start()
-    for side in range(2):
-        for i in range(tab_parts):
-            tab_copy(side, i).start()
-
     out_row = lax.broadcasted_iota(jnp.int32, (group_rows, group_rows), 0)
     in_row = lax.broadcasted_iota(jnp.int32, (group_rows, group_rows), 1)
     wanted = (out_row % group_levels) * rows_ky + out_row // group_levels
@@ -129,8 +126,6 @@
             device_id_type=MESH,
         )
 
-    has_prev = (q + chain - 1) // chain
-    has_next = (2 * chain - 2 - q) // chain
     pl.semaphore_wait(barrier, lev + has_prev + has_next)
     to_prev = pltpu.make_async_remote_copy(
         src_ref=x_ref.at[2, :, 0:halo_rows],
@@ -150,6 +145,7 @@
     )
     to_next.start()
     to_prev.start()
+
     first_unit, first_way = unit(0)
     for c in range(2):
         x_copy(0, c).wait()
@@ -165,6 +161,9 @@
         zpad[c, rows_ky:rows_ky + line_rows, :] = x_buf[2, c].astype(f32)
     for c in range(2):
         x_copy(1, c).wait()
+    for side in range(2):
+        for i in range(tab_parts):
+            tab_copy(side, i).start()
     ky_row = lax.broadcasted_iota(jnp.int32, (group_rows, chunk), 0) % rows_ky
     ky_scaled = ky_row.astype(f32) * spacing
     for part_of in range(2):
@@ -191,11 +190,14 @@
         if part_of == 0:
             line_copy(first_unit, 0, 1).start()
 
-    def send_lines(s, carry):
-        d, _ = unit(s)
+    def start_lines(d):
         for which in range(2):
             for g in range(2):
                 line_copy(d, which, g).start()
+
+    def send_lines(s, carry):
+        d, _ = unit(s)
+        start_lines(d)
         return carry
 
     lax.fori_loop(1, chain, send_lines, 0)
@@ -261,20 +263,19 @@
 
     norm_scale = 1.0 / math.sqrt(NXG)
 
-    def transform(d, k, begin, n):
+    def transform(target, k, begin, n, holders, table):
         rows = slice(begin, begin + n)
         lines = jnp.concatenate(
-            [
-                send[2 * d + h, :, rows, :].reshape(4 * n, chunk),
-                recv[d, :, rows, :].reshape(4 * n, chunk),
-            ],
-            axis=1,
+            [holder[:, rows, :].reshape(4 * n, chunk) for holder in holders], axis=1
         )
         for t in range(SEC // TILE):
             first = k * SEC + t * TILE
-            with_cos = jnp.dot(lines, tab[:, first:first + TILE], preferred_element_type=f32)
+            cos_at, sin_at = pl.multiple_of(first, TILE), pl.multiple_of(KXM + first, TILE)
+            with_cos = jnp.dot(
+                lines, table[:, pl.ds(cos_at, TILE)], preferred_element_type=f32
+            )
             with_sin = jnp.dot(
-                lines, tab[:, KXM + first:KXM + first + TILE], preferred_element_type=f32
+                lines, table[:, pl.ds(sin_at, TILE)], preferred_element_type=f32
             )
             kx = (
                 lax.broadcasted_iota(jnp.int32, (1, TILE), 1) + first - KXM // 2
@@ -287,9 +288,13 @@
             source_imag = -kx * fx_real - fg_imag
             for j in range(TILE // 128):
                 at = slice(j * 128, (j + 1) * 128)
-                row = begin * DEEP + t * (TILE // 128) + j
-                part[k, pl.ds(row, n, stride=DEEP), :] = source_real[:, at]
-                part[k, pl.ds(PER + row, n, stride=DEEP), :] = source_imag[:, at]
+                place_at = begin * DEEP + t * (TILE // 128) + j
+                for c, source in ((0, source_real), (1, source_imag)):
+                    where = pl.ds(c * PER + place_at, n, stride=DEEP)
+                    target[k, where, :] = source[:, at]
+
+    def transform_unit(d, k, begin, n):
+        transform(part, k, begin, n, [send.at[2 * d + h], recv.at[d]], tab)
 
     flow_rows = (pl.ds(0, half_levels * DEEP), pl.ds(half_levels * DEEP, (half_levels + 2) * DEEP))
 
@@ -373,7 +378,7 @@
     for g in range(2):
         await_lines(first_unit, g)
         for k in range(SECTIONS):
-            transform(first_unit, k, g * half_levels, half_levels)
+            transform_unit(first_unit, k, g * half_levels, half_levels)
             await_flow(first_unit, first_way, k, g)
             if g == 0:
                 lost, older = shape_noise(first_unit, k, g, (zeros, zeros))
@@ -383,129 +388,158 @@
                 shape_noise(first_unit, k, g, (lost_val[k, 0], lost_val[k, 1]))
             flow_copy(first_unit, first_way, k, g).start()
 
-    def pass_on(s, carry):
-        d, way = unit(s)
-        await_lines(d, 0)
-        await_lines(d, 1)
+    def pass_unit(d, way):
         for k in range(SECTIONS):
-            transform(d, k, 0, levels)
+            transform_unit(d, k, 0, levels)
             lost = (zeros, zeros)
             for g in range(2):
                 await_flow(d, way, k, g)
                 lost = shape_noise(d, k, g, lost)
                 flow_copy(d, way, k, g).start()
+
+    def pass_on(s, carry):
+        d, way = unit(s)
+        await_lines(d, 0)
+        await_lines(d, 1)
+        pass_unit(d, way)
         return carry
 
     lax.fori_loop(1, chain - 1, pass_on, 0)
-
     await_lines(q, 0)
     await_lines(q, 1)
-    for k in range(SECTIONS):
-        transform(q, k, 0, levels)
-
-    def end_copy(step, slot, k):
+
+    @pl.loop(0, SECTIONS)
+    def _(k):
+        transform(own_part, k, 0, levels, [send.at[me], recv.at[q]], tab)
+
+    section_groups = (range(SECTIONS - 1), range(SECTIONS - 1, SECTIONS))
+
+    def end_copy(step, slot, n):
+        sections = pl.ds(section_groups[n][0], len(section_groups[n]))
         return pltpu.make_async_remote_copy(
-            src_ref=ends.at[slot, k],
-            dst_ref=ends.at[slot, k],
-            send_sem=end_send.at[step, k],
-            recv_sem=end_recv.at[step, k],
+            src_ref=ends.at[slot, sections],
+            dst_ref=ends.at[slot, sections],
+            send_sem=end_send.at[step, n],
+            recv_sem=end_recv.at[step, n],
             device_id={"lev": (block + step) % lev},
             device_id_type=MESH,
         )
 
-    def down_pass(k):
+    def down_pass(n):
+        sections = section_groups[n]
+
         def down_pair(i, carry):
-            value, first = carry
             rows = level_rows(2 * i, 2)
-            both = part[k, rows, :] + (
-                flow_in[q, k, rows, :].astype(f32) + flow_in[chain, k, rows, :].astype(f32)
-            )
-            weighted = from_lo[k, rows, :] * both
-            first = first + (weighted[:DEEP] + weighted[DEEP:])
-            inverse = coef[k, rows, :]
-            low = (both[:DEEP] + value) * inverse[:DEEP]
-            high = (both[DEEP:] + low) * inverse[DEEP:]
-            part[k, rows, :] = jnp.concatenate([low, high], axis=0)
-            return high, first
-
-        carry = (zeros, zeros)
+            after = []
+            for i_k, k in enumerate(sections):
+                value, first = carry[2 * i_k], carry[2 * i_k + 1]
+                both = own_part[k, rows, :] + (
+                    flow_in[q, k, rows, :].astype(f32) + flow_in[chain, k, rows, :].astype(f32)
+                )
+                weighted = from_lo[k, rows, :] * both
+                first = first + (weighted[:DEEP] + weighted[DEEP:])
+                inverse = coef[k, rows, :]
+                low = (both[:DEEP] + value) * inverse[:DEEP]
+                high = (both[DEEP:] + low) * inverse[DEEP:]
+                own_part[k, rows, :] = jnp.concatenate([low, high], axis=0)
+                after += [high, first]
+            return tuple(after)
+
+        carry = (zeros, zeros) * len(sections)
         for g in range(2):
-            @pl.when(q > 0)
-            def _():
-                arrival(q, k, g).wait_recv()
-
-            @pl.when(q < chain - 1)
-            def _():
-                arrival(chain, k, g).wait_recv()
-
-            if g == 1:
-                rows, rest = pl.ds((levels - 2) * DEEP, 2 * DEEP), pl.ds(levels * DEEP, 2 * DEEP)
-                part[k, rows, :] = part[k, rows, :] + (
-                    flow_in[q, k, rest, :].astype(f32) + flow_in[chain, k, rest, :].astype(f32)
+            for k in sections:
+                @pl.when(q > 0)
+                def _():
+                    arrival(q, k, g).wait_recv()
+
+                @pl.when(q < chain - 1)
+                def _():
+                    arrival(chain, k, g).wait_recv()
+
+                if g == 1:
+                    rows = pl.ds((levels - 2) * DEEP, 2 * DEEP)
+                    rest = pl.ds(levels * DEEP, 2 * DEEP)
+                    own_part[k, rows, :] = own_part[k, rows, :] + (
+                        flow_in[q, k, rest, :].astype(f32)
+                        + flow_in[chain, k, rest, :].astype(f32)
+                    )
+            carry = over_pairs(down_pair, g * half_pairs, half_pairs, carry)
+        for i_k, k in enumerate(sections):
+            ends[block, k, 0:DEEP, :] = carry[2 * i_k + 1]
+            ends[block, k, DEEP:2 * DEEP, :] = carry[2 * i_k]
+        for step in range(1, lev):
+            end_copy(step, block, n).start()
+
+    def up_pass(n):
+        sections = section_groups[n]
+        nears, distants, ratios, inverses, leads = [], [], [], [], []
+        for k in sections:
+            near = from_lo[k, 0:DEEP, :]
+            distant = from_lo[k, (levels - 1) * DEEP:levels * DEEP, :]
+            ratio = near
+            some_ratios, some_inverses, some_leads = [ratio], [None], [None]
+            for b in range(1, lev):
+                inverse = 1.0 / (1.0 - near * ratio)
+                lead = distant * ratio * inverse
+                ratio = near + lead * distant
+                some_ratios.append(ratio)
+                some_inverses.append(inverse)
+                some_leads.append(lead)
+            nears.append(near)
+            distants.append(distant)
+            ratios.append(some_ratios)
+            inverses.append(some_inverses)
+            leads.append(some_leads)
+        for step in range(1, lev):
+            end_copy(step, (block + lev - step) % lev, n).wait_recv()
+        for i_k, k in enumerate(sections):
+            near, distant = nears[i_k], distants[i_k]
+            value = ends[0, k, DEEP:2 * DEEP, :]
+            values = [value]
+            for b in range(1, lev):
+                first = ends[b, k, 0:DEEP, :] + near * value
+                value = ends[b, k, DEEP:2 * DEEP, :] + distant * value + leads[i_k][b] * first
+                values.append(value)
+            follow = zeros
+            first_val[lev, k] = follow
+            last_val[0, k] = follow
+            for b in range(lev - 1, 0, -1):
+                follow = inverses[i_k][b] * (
+                    ends[b, k, 0:DEEP, :] + near * values[b - 1] + distant * follow
                 )
-            carry = over_pairs(down_pair, g * half_pairs, half_pairs, carry)
-        value, first = carry
-        ends[block, k, 0:DEEP, :] = first
-        ends[block, k, DEEP:2 * DEEP, :] = value
-        for step in range(1, lev):
-            end_copy(step, block, k).start()
-
-    def up_pass(k):
-        near = from_lo[k, 0:DEEP, :]
-        distant = from_lo[k, (levels - 1) * DEEP:levels * DEEP, :]
-        ratio = near
-        ratios, inverses, leads = [ratio], [None], [None]
-        for b in range(1, lev):
-            inverse = 1.0 / (1.0 - near * ratio)
-            lead = distant * ratio * inverse
-            ratio = near + lead * distant
-            ratios.append(ratio)
-            inverses.append(inverse)
-            leads.append(lead)
-        for step in range(1, lev):
-            end_copy(step, (block + lev - step) % lev, k).wait_recv()
-        value = ends[0, k, DEEP:2 * DEEP, :]
-        values = [value]
-        for b in range(1, lev):
-            first = ends[b, k, 0:DEEP, :] + near * value
-            value = ends[b, k, DEEP:2 * DEEP, :] + distant * value + leads[b] * first
-            values.append(value)
-        follow = zeros
-        first_val[lev] = follow
-        last_val[0] = follow
-        for b in range(lev - 1, 0, -1):
-            follow = inverses[b] * (
-                ends[b, k, 0:DEEP, :] + near * values[b - 1] + distant * follow
-            )
-            first_val[b] = follow
-            last_val[b] = values[b - 1] + ratios[b - 1] * follow
-        below = last_val[block]
+                first_val[b, k] = follow
+                last_val[b, k] = values[b - 1] + ratios[i_k][b - 1] * follow
+        below = [last_val[block, k] for k in sections]
 
         def up_pair(j, carry):
             rows = level_rows(levels - 2 - 2 * j, 2)
-            both, inverse = part[k, rows, :], coef[k, rows, :]
-            high = both[DEEP:] + inverse[DEEP:] * carry
-            low = both[:DEEP] + inverse[:DEEP] * high
-            gain = from_lo[k, rows, :]
-            part[k, rows, :] = jnp.concatenate(
-                [low + gain[:DEEP] * below, high + gain[DEEP:] * below], axis=0
-            )
-            return low
-
-        over_pairs(up_pair, 0, levels // 2, first_val[block + 1])
+            after = []
+            for i_k, k in enumerate(sections):
+                both, inverse = own_part[k, rows, :], coef[k, rows, :]
+                high = both[DEEP:] + inverse[DEEP:] * carry[i_k]
+                low = both[:DEEP] + inverse[:DEEP] * high
+                gain = from_lo[k, rows, :]
+                own_part[k, rows, :] = jnp.concatenate(
+                    [low + gain[:DEEP] * below[i_k], high + gain[DEEP:] * below[i_k]], axis=0
+                )
+                after.append(low)
+            return tuple(after)
+
+        over_pairs(
+            up_pair, 0, levels // 2, tuple(first_val[block + 1, k] for k in sections)
+        )
         tiles = KXM // 128
-        for c in range(2):
-            for j in range(PER):
-                out_ref[pl.ds(c * levels * tiles + k * PER + j, levels, stride=tiles), :] = part[
-                    k, pl.ds(c * PER + j, levels, stride=DEEP), :
-                ]
-
-    for k in range(SECTIONS):
-        down_pass(k)
-        if k > 0 and k < SECTIONS - 1:
-            up_pass(k - 1)
-    for k in range(max(SECTIONS - 2, 0), SECTIONS):
-        up_pass(k)
+        for k in sections:
+            for c in range(2):
+                for j in range(PER):
+                    out_ref[pl.ds(c * levels * tiles + k * PER + j, levels, stride=tiles), :] = (
+                        own_part[k, pl.ds(c * PER + j, levels, stride=DEEP), :]
+                    )
+
+    for n in range(len(section_groups)):
+        down_pass(n)
+    for n in range(len(section_groups)):
+        up_pass(n)
 
     to_prev.wait_send()
     to_next.wait_send()
@@ -526,9 +560,9 @@
         return carry
 
     lax.fori_loop(0, chain - 1, flows_sent, 0)
-    for k in range(SECTIONS):
+    for n in range(len(section_groups)):
         for step in range(1, lev):
-            end_copy(step, block, k).wait_send()
+            end_copy(step, block, n).wait_send()
 
 
 def solution(mesh):
@@ -559,13 +593,14 @@
                 pltpu.VMEM((2, halo_rows, chunk), bf16),
                 pltpu.VMEM((2, rows + 2 * rows_ky, chunk), f32),
                 pltpu.VMEM((SECTIONS, levels * DEEP, 128), f32),
+                pltpu.VMEM((SECTIONS, levels * DEEP, 128), f32),
                 pltpu.VMEM((chain, SECTIONS, (levels + 2) * DEEP, 128), bf16),
                 pltpu.VMEM((chain + 1, SECTIONS, (levels + 2) * DEEP, 128), bf16),
                 pltpu.VMEM((SECTIONS, levels * DEEP, 128), f32),
                 pltpu.VMEM((SECTIONS, levels * DEEP, 128), f32),
                 pltpu.VMEM((lev, SECTIONS, 2 * DEEP, 128), f32),
-                pltpu.VMEM((lev + 1, DEEP, 128), f32),
-                pltpu.VMEM((lev + 1, DEEP, 128), f32),
+                pltpu.VMEM((lev + 1, SECTIONS, DEEP, 128), f32),
+                pltpu.VMEM((lev + 1, SECTIONS, DEEP, 128), f32),
                 pltpu.VMEM((SECTIONS, 2, DEEP, 128), f32),
                 dma((3, 2)),
                 dma((2, 4)),
@@ -575,8 +610,8 @@
                 dma((2, 2, chain)),
                 dma((chain, SECTIONS, 2)),
                 dma((chain + 1, SECTIONS, 2)),
-                dma((lev, SECTIONS)),
-                dma((lev, SECTIONS)),
+                dma((lev, 2)),
+                dma((lev, 2)),
             ],
             compiler_params=pltpu.CompilerParams(
                 collective_id=0, has_side_effects=True, vmem_limit_bytes=56 * 2**20

time: 42.3 us -> 41.6 us (0.983)
  Pallas kernels: 41.3 us -> 40.6 us
    pallas_call x1, Pallas kernels: 41.3 us -> 40.6 us  [local(): pl.pallas_call(functools.partial(kernel, wide, lev, rows_ky, levels), out...]
where the time goes in v3:
time: 41.6 us; the launch traced here: 41.5 us
  Pallas kernels  40.6 us (98%)
  local copies, waits for them, and re-layouts  0.88 us (2%)
    pallas_call x1, Pallas kernels, local(): pl.pallas_call(functools.partial(kernel, wide, lev, rows_ky, levels), out...  40.6 us
    unnamed x1, local copies, waits for them, and re-layouts  0.88 us

profile of v3, /device:TPU:17, one launch (start us, length us, event | category | flops | bytes accessed | tf_op | source)
XLA Modules:
  0.0 41.5 jit_solution(1851808130557124536)
XLA Ops:
  0.0 40.6 %shard_map.28 = f32[1536,128]{1,0:T(8,128)S(1)} custom-call(bf16[3,2,512,512]{3,2,1,0:T(8,128)(2,1)} %bitcast.3, bf16[4096,3072]{1,0:T(8,128)(2,1)} %constant.2.clone.tab_ref), custom_call_target="tpu_custom_call" | custom-call | flops 6442450944 | bytes 8388608 | tf_op jit(solution)/shard_map/pallas_call | solution.py:579
  40.6 0.9 %copy.5 = f32[2,64,1,1536]{3,2,1,0:T(1,128)} copy(f32[2,64,1,1536]{3,2,1,0:T(1,128)S(1)} %bitcast.2) | data formatting | bytes 1572864

commit v4 on v3

--- a/solution.py
+++ b/solution.py
@@ -296,13 +296,18 @@
     def transform_unit(d, k, begin, n):
         transform(part, k, begin, n, [send.at[2 * d + h], recv.at[d]], tab)
 
-    flow_rows = (pl.ds(0, half_levels * DEEP), pl.ds(half_levels * DEEP, (half_levels + 2) * DEEP))
+    def has_rest(k):
+        return k * SEC < KXM // 2 < (k + 1) * SEC
+
+    def flow_rows(k, g):
+        return pl.ds(g * half_levels * DEEP, (half_levels + 2 * (g * has_rest(k))) * DEEP)
+
 
     def flow_copy(d, way, k, g):
         slot = jnp.where(q + way == d, jnp.where(way > 0, d, chain), d)
         return pltpu.make_async_remote_copy(
-            src_ref=flow_out.at[d, k, flow_rows[g]],
-            dst_ref=flow_in.at[slot, k, flow_rows[g]],
+            src_ref=flow_out.at[d, k, flow_rows(k, g)],
+            dst_ref=flow_in.at[slot, k, flow_rows(k, g)],
             send_sem=flow_send.at[d, k, g],
             recv_sem=flow_recv.at[slot, k, g],
             device_id={"wide": me + 2 * way},
@@ -311,8 +316,8 @@
 
     def arrival(slot, k, g):
         return pltpu.make_async_remote_copy(
-            src_ref=flow_out.at[0, k, flow_rows[g]],
-            dst_ref=flow_in.at[slot, k, flow_rows[g]],
+            src_ref=flow_out.at[0, k, flow_rows(k, g)],
+            dst_ref=flow_in.at[slot, k, flow_rows(k, g)],
             send_sem=flow_send.at[0, k, g],
             recv_sem=flow_recv.at[slot, k, g],
             device_id={"wide": pair},
@@ -354,6 +359,8 @@
 
         if g == 0:
             return over_pairs(one_pair, 0, half_pairs, carry)
+        if not has_rest(k):
+            return over_pairs(one_pair, half_pairs, half_pairs, carry)
         lost, older = over_pairs(one_pair, half_pairs, half_pairs - 1, carry)
         rows, rest = pl.ds((levels - 2) * DEEP, 2 * DEEP), pl.ds(levels * DEEP, 2 * DEEP)
         both = part[k, rows, :] + flow_in[d, k, rows, :].astype(f32)
@@ -456,7 +463,7 @@
                 def _():
                     arrival(chain, k, g).wait_recv()
 
-                if g == 1:
+                if g == 1 and has_rest(k):
                     rows = pl.ds((levels - 2) * DEEP, 2 * DEEP)
                     rest = pl.ds(levels * DEEP, 2 * DEEP)
                     own_part[k, rows, :] = own_part[k, rows, :] + (

time: 41.6 us -> 41.1 us (0.988)
  Pallas kernels: 40.6 us -> 40 us
    pallas_call x1, Pallas kernels: 40.6 us -> 40 us  [local(): pl.pallas_call(functools.partial(kernel, wide, lev, rows_ky, levels), out...]
where the time goes in v4:
time: 41.1 us; the launch traced here: 40.9 us
  Pallas kernels  40 us (97%)
  local copies, waits for them, and re-layouts  0.88 us (2%)
    pallas_call x1, Pallas kernels, local(): pl.pallas_call(functools.partial(kernel, wide, lev, rows_ky, levels), out...  40 us
    unnamed x1, local copies, waits for them, and re-layouts  0.88 us

profile of v4, /device:TPU:17, one launch (start us, length us, event | category | flops | bytes accessed | tf_op | source)
XLA Modules:
  0.0 40.9 jit_solution(5143312755758213872)
XLA Ops:
  0.0 40.0 %shard_map.28 = f32[1536,128]{1,0:T(8,128)S(1)} custom-call(bf16[3,2,512,512]{3,2,1,0:T(8,128)(2,1)} %bitcast.3, bf16[4096,3072]{1,0:T(8,128)(2,1)} %constant.2.clone.tab_ref), custom_call_target="tpu_custom_call" | custom-call | flops 6442450944 | bytes 8388608 | tf_op jit(solution)/shard_map/pallas_call | solution.py:586
  40.1 0.9 %copy.5 = f32[2,64,1,1536]{3,2,1,0:T(1,128)} copy(f32[2,64,1,1536]{3,2,1,0:T(1,128)S(1)} %bitcast.2) | data formatting | bytes 1572864

commit v5 on v4

--- a/solution.py
+++ b/solution.py
@@ -14,7 +14,7 @@
 KXM = 1536
 MESH = pl.DeviceIdType.MESH
 SEC = 512
-TILE = 256
+TILE = 512
 SECTIONS = KXM // SEC
 PER = SEC // 128
 DEEP = 2 * PER
@@ -149,16 +149,17 @@
     first_unit, first_way = unit(0)
     for c in range(2):
         x_copy(0, c).wait()
-    for part_of in range(2):
+
+    def place_x(part_of):
         for g in range(part_of * groups // 2, (part_of + 1) * groups // 2):
             for c in range(2):
                 place(x_buf[0, c, g * group_rows:(g + 1) * group_rows, :], c, g)
-        if part_of == 0:
-            line_copy(first_unit, 0, 0).start()
+        line_copy(first_unit, 0, part_of).start()
+
+    place_x(0)
 
     for c in range(2):
         x_copy(2, c).wait()
-        zpad[c, rows_ky:rows_ky + line_rows, :] = x_buf[2, c].astype(f32)
     for c in range(2):
         x_copy(1, c).wait()
     for side in range(2):
@@ -166,7 +167,11 @@
             tab_copy(side, i).start()
     ky_row = lax.broadcasted_iota(jnp.int32, (group_rows, chunk), 0) % rows_ky
     ky_scaled = ky_row.astype(f32) * spacing
+    early_rows = (half_levels + 2) * rows_ky
     for part_of in range(2):
+        begin, end = ((0, early_rows), (early_rows, line_rows))[part_of]
+        for c in range(2):
+            zpad[c, rows_ky + begin:rows_ky + end, :] = x_buf[2, c, begin:end, :].astype(f32)
         if part_of == 0:
             to_next.wait_recv()
             for c in range(2):
@@ -188,7 +193,7 @@
                 place(mixed.astype(bf16), 2 + c, g)
         line_copy(first_unit, 1, part_of).start()
         if part_of == 0:
-            line_copy(first_unit, 0, 1).start()
+            place_x(1)
 
     def start_lines(d):
         for which in range(2):
@@ -325,7 +330,7 @@
         )
 
     def over_pairs(body, begin, count, carry):
-        group = max(n for n in range(1, 9) if count % n == 0)
+        group = max(n for n in range(1, 17) if count % n == 0)
 
         def some(j, carry):
             for i in range(group):

time: 41.1 us -> 41 us (level)
  no operation moved by 1% of the time
where the time goes in v5:
time: 41 us; the launch traced here: 40.9 us
  Pallas kernels  40 us (98%)
  local copies, waits for them, and re-layouts  0.88 us (2%)
    pallas_call x1, Pallas kernels, local(): pl.pallas_call(functools.partial(kernel, wide, lev, rows_ky, levels), out...  40 us
    unnamed x1, local copies, waits for them, and re-layouts  0.88 us

profile of v5, /device:TPU:17, one launch (start us, length us, event | category | flops | bytes accessed | tf_op | source)
XLA Modules:
  0.0 40.9 jit_solution(9322541324383860407)
XLA Ops:
  0.0 40.0 %shard_map.28 = f32[1536,128]{1,0:T(8,128)S(1)} custom-call(bf16[3,2,512,512]{3,2,1,0:T(8,128)(2,1)} %bitcast.3, bf16[4096,3072]{1,0:T(8,128)(2,1)} %constant.2.clone.tab_ref), custom_call_target="tpu_custom_call" | custom-call | flops 6442450944 | bytes 8388608 | tf_op jit(solution)/shard_map/pallas_call | solution.py:591
  40.0 0.9 %copy.5 = f32[2,64,1,1536]{3,2,1,0:T(1,128)} copy(f32[2,64,1,1536]{3,2,1,0:T(1,128)S(1)} %bitcast.2) | data formatting | bytes 1572864
